TPU v7x, 32 devices: a whole 2x2x4 slice. The times are simulated.
32 devices in a mesh: level: 2 (over y), lon: 8 (over z, x), lat: 2 (over core).
Axes of the slice: x: 2, y: 2, z: 4, core: 2. Of those that a mesh axis runs over, the one named last changes fastest.
Arguments:
- wind_snaps: float32 [4, 32, 32, 256], P('level', None, 'lon', 'lat'), parts along dimension 0, may hold values from -48 to 48
- old_basis: float32 [4, 64, 32, 256], P('level', None, 'lon', 'lat'), parts along dimension 0, may hold values from -17 to 17
- old_values: float32 [4, 64], P('level'), parts along dimension 0, may hold values from 1 to 4
Outputs:
- new_basis: float32 [4, 64, 32, 256], P('level', None, 'lon', 'lat'), parts along dimension 0
- new_values: float32 [4, 64], P('level'), parts along dimension 0
There are 2 independent parts, one for each index of `level`. A program takes and returns all parts, laid end to end along the dimension named above; each array names one. Nothing has to cross between parts.
All inputs are finite; a program needn't handle non-finite values.
Results may differ from a plain program's by a relative error of at most 0.00012.
Values sent between devices are 32-bit elements; how exact they have to be, the bound alone decides.
A program may use at most 64 MiB of HBM per device.

v0:
```python
import jax
import jax.numpy as jnp
from jax import lax
from jax.sharding import PartitionSpec as P

ITERS = 2
FULL_PRECISION = lax.Precision.HIGHEST


def extended(value, sides, width, wrap):
    for axis, dim in sides:
        count, length = (lax.axis_size(axis), value.shape[dim])
        up = [(i, (i + 1) % count) for i in range(count if wrap else count - 1)]
        down = [(j, i) for i, j in up]
        last = lax.slice_in_dim(value, length - width, length, axis=dim)
        first = lax.slice_in_dim(value, 0, width, axis=dim)
        before = lax.ppermute(last, axis, up)
        after = lax.ppermute(first, axis, down)
        value = jnp.concatenate([before, value, after], axis=dim)
    return value


def cholesky_pair(matrix):
    order = matrix.shape[0]
    positions = jnp.arange(order, dtype=jnp.int32)

    def row_step(row, carry):
        lower, inverse = carry
        column = lax.dynamic_slice_in_dim(matrix, row, 1, 1)[:, 0]
        partial_row = jnp.dot(inverse, column, precision=FULL_PRECISION)
        diag_entry = lax.dynamic_slice_in_dim(column, row, 1, 0)[0]
        pivot = jnp.sqrt(diag_entry - jnp.sum(partial_row * partial_row))
        unit = (positions == row).astype(matrix.dtype)
        lower_row = partial_row + pivot * unit
        inverse_row = (unit - jnp.dot(partial_row, inverse, precision=FULL_PRECISION)) / pivot
        lower = lax.dynamic_update_slice_in_dim(lower, lower_row[None], row, 0)
        inverse = lax.dynamic_update_slice_in_dim(inverse, inverse_row[None], row, 0)
        return (lower, inverse)

    return lax.fori_loop(0, order, row_step, (jnp.zeros_like(matrix), jnp.zeros_like(matrix)))


def project_one(gram_uu, gram_ua):
    factor_low, low_inverse = cholesky_pair(gram_uu)
    projected = jnp.dot(low_inverse, gram_ua, precision=FULL_PRECISION)
    lifted = jnp.dot(low_inverse.T, projected, precision=FULL_PRECISION)
    return (low_inverse, projected, lifted)


def upper_pair(gram):
    lower, inverse = cholesky_pair(gram)
    return (lower.T, inverse.T)


def rotate_one(low_inverse, projected, factor_up, up_inverse, values):
    rank_count = values.shape[0]
    snap_count = factor_up.shape[0]
    top_rows = jnp.concatenate([jnp.diag(values), projected], axis=1)
    bottom_rows = jnp.concatenate(
        [jnp.zeros((snap_count, rank_count), jnp.float32), factor_up], axis=1
    )
    joint_matrix = jnp.concatenate([top_rows, bottom_rows], axis=0)
    square = jnp.dot(joint_matrix, joint_matrix.T, precision=FULL_PRECISION)
    subspace = jnp.eye(rank_count + snap_count, rank_count, dtype=jnp.float32)
    for sweep in range(ITERS):
        applied = jnp.dot(square, subspace, precision=FULL_PRECISION)
        inner = jnp.dot(applied.T, applied, precision=FULL_PRECISION)
        chol_low, chol_inverse = cholesky_pair(inner)
        subspace = jnp.dot(applied, chol_inverse.T, precision=FULL_PRECISION)
    energy = jnp.sum(subspace * jnp.dot(square, subspace, precision=FULL_PRECISION), axis=0)
    new_values = jnp.sqrt(energy)
    mix_old = jnp.dot(low_inverse.T, subspace[:rank_count], precision=FULL_PRECISION).T
    mix_new = jnp.dot(up_inverse, subspace[rank_count:], precision=FULL_PRECISION).T
    return (mix_old, mix_new, new_values)


def residual_rows(fields, basis_rows, lifted):
    return fields - jnp.einsum("fks,fkc->fsc", lifted, basis_rows, precision=FULL_PRECISION)


def per_device(wind_snaps, old_basis, old_values):
    snap_count = wind_snaps.shape[1]
    rank_count = old_basis.shape[1]
    lon_cells = wind_snaps.shape[2]
    lat_cells = wind_snaps.shape[3]
    rows_all = lat_cells * lax.axis_size("lat")
    cell_count = lon_cells * lax.axis_size("lon") * rows_all
    row_place = (lax.axis_index("lat") * lat_cells + jnp.arange(lat_cells, dtype=jnp.int32)).astype(
        jnp.float32
    )
    cosines = jnp.cos(((row_place + 0.5) / rows_all - 0.5) * (jnp.pi / 2.0))
    lon_padded = extended(wind_snaps, (("lon", 2),), 1, True)
    lat_padded = extended(wind_snaps * cosines, (("lat", 3),), 1, False)
    lon_diff = lon_padded[:, :, 2:, :] - lon_padded[:, :, :-2, :]
    lat_diff = lat_padded[:, :, :, 2:] - lat_padded[:, :, :, :-2]
    twice_cos = 2.0 * cosines
    vorticity = (lon_diff[1] - lat_diff[0]) / twice_cos
    divergence = (lon_diff[0] + lat_diff[1]) / twice_cos
    fields = jnp.stack([vorticity, divergence]).reshape(2, snap_count, lon_cells * lat_cells)
    basis_rows = old_basis.reshape(2, rank_count, lon_cells * lat_cells)
    local_uu = jnp.einsum("fkc,fjc->fkj", basis_rows, basis_rows, precision=FULL_PRECISION)
    local_ua = jnp.einsum("fkc,fsc->fks", basis_rows, fields, precision=FULL_PRECISION)
    sum_uu, sum_ua = lax.psum((local_uu, local_ua), ("lon", "lat"))
    low_inverse, projected, lifted = jax.vmap(project_one)(sum_uu / cell_count, sum_ua / cell_count)
    residual = residual_rows(fields, basis_rows, lifted)
    local_rr = jnp.einsum("fsc,ftc->fst", residual, residual, precision=FULL_PRECISION)
    sum_rr = lax.psum(local_rr, ("lon", "lat"))
    factor_up, up_inverse = jax.vmap(upper_pair)(sum_rr / cell_count)
    mix_old, mix_new, new_values = jax.vmap(rotate_one)(
        low_inverse, projected, factor_up, up_inverse, old_values
    )
    new_basis = jnp.einsum("fkj,fjc->fkc", mix_old, basis_rows, precision=FULL_PRECISION)
    new_basis = new_basis + jnp.einsum("fks,fsc->fkc", mix_new, residual, precision=FULL_PRECISION)
    return (new_basis.reshape(2, rank_count, lon_cells, lat_cells), new_values)


def solution(mesh):
    placed = (P("level", None, "lon", "lat"), P("level", None, "lon", "lat"), P("level", None))
    return jax.shard_map(
        per_device,
        mesh=mesh,
        in_specs=placed,
        out_specs=(P("level", None, "lon", "lat"), P("level", None)),
        check_vma=False,
    )
```

profile of v0, /device:TPU:0, one launch (start us, length us, event | category | flops | bytes accessed | tf_op | source)
XLA Modules:
  0.0 1083.0 jit_solution(2098849238049554596)
XLA Ops:
  0.6 1.0 fusion.76
  1.7 6.0 collective-permute-start
  7.7 1.1 reshape.448
  10.0 4.3 collective-permute-done.1
  14.3 1.2 fusion.47
  15.7 1.3 collective-permute-start.2
  17.0 3.0 collective-permute-start.3
  20.1 0.9 collective-permute-done.3
  21.7 58.7 %all-reduce.1 = (f32[2,64,64]{2,1,0:T(8,128)S(1)}, f32[2,64,32]{1,2,0:T(8,128)S(1)}) all-reduce(f32[2,64,64]{2,1,0:T(8,128)S(1)} %fusion.78, f32[2,64,32]{1,2,0:T(8,128)S(1)} %convolution_bitcast_fusion), channel_id=1, replica_groups=mesh['level'=2,'lon'=8,'lat'=2] {'lon','lat'}, use_global_device_ids=true, to_apply=%region_0.0 | all-reduce | flops 12288 | bytes 98304 | tf_op jit(solution)/shard_map/psum | solution.py:103
  81.2 268.9 %while.71 = (s32[]{:T(128)}, f32[2,64,64]{2,0,1:T(2,128)S(1)}, f32[2,64,64]{0,2,1:T(8,128)S(1)}, s32[]{:T(128)}, s32[2]{0:T(128)S(1)}, /*index=5*/s32[1]{0:T(128)}, s32[3]{0:T(128)S(1)}, s32[]{:T(128)}, s32[]{:T(128)}) while((s32[]{:T(128)}, f32[2,64,64]{2,0,1:T(2,128)S(1)}, f32[2,64,64]{0,2,1:T(8,128)S(1)}, s32[]{:T(128)}, ...), condition=%wide.region_4.5_spmd.clone, body=%wide.region_1.4_spmd.clone.sunk | while | flops 197400 | bytes 75255 | solution.py:40
  351.3 57.6 %psum.23 = f32[2,32,32]{2,1,0:T(8,128)S(1)} all-reduce(f32[2,32,32]{2,1,0:T(8,128)S(1)} %fusion.80), channel_id=1, replica_groups=mesh['level'=2,'lon'=8,'lat'=2] {'lon','lat'}, use_global_device_ids=true, to_apply=%region_6.0 | all-reduce | flops 2048 | bytes 16384 | tf_op jit(solution)/shard_map/psum | solution.py:107
  409.3 131.4 %while.72 = (s32[]{:T(128)}, f32[2,32,32]{2,0,1:T(2,128)S(1)}, f32[2,32,32]{2,0,1:T(2,128)S(1)}, f32[2,32,32]{0,2,1:T(8,128)S(1)}, s32[]{:T(128)}, /*index=5*/s3...) while((s32[]{:T(128)}, f32[2,32,32]{2,0,1:T(2,128)S(1)}, ...), condition=%wide.region_10.11_spmd.clone, body=%wide.region_7.10_spmd.clone.sunk | while | flops 49752 | bytes 26751 | solution.py:40
  412.6 0.8 constant_dynamic-update-slice_fusion.5
  416.7 0.8 constant_dynamic-update-slice_fusion.5
  420.8 0.8 constant_dynamic-update-slice_fusion.5
  424.9 0.8 constant_dynamic-update-slice_fusion.5
  429.0 0.8 constant_dynamic-update-slice_fusion.5
  433.1 0.8 constant_dynamic-update-slice_fusion.5
  437.2 0.8 constant_dynamic-update-slice_fusion.5
  441.4 0.8 constant_dynamic-update-slice_fusion.5
  445.5 0.8 constant_dynamic-update-slice_fusion.5
  449.6 0.8 constant_dynamic-update-slice_fusion.5
  453.7 0.8 constant_dynamic-update-slice_fusion.5
  457.8 0.8 constant_dynamic-update-slice_fusion.5
  461.9 0.8 constant_dynamic-update-slice_fusion.5
  466.0 0.8 constant_dynamic-update-slice_fusion.5
  470.1 0.8 constant_dynamic-update-slice_fusion.5
  474.2 0.8 constant_dynamic-update-slice_fusion.5
  478.3 0.8 constant_dynamic-update-slice_fusion.5
  482.4 0.8 constant_dynamic-update-slice_fusion.5
  486.5 0.8 constant_dynamic-update-slice_fusion.5
  490.6 0.8 constant_dynamic-update-slice_fusion.5
  494.7 0.8 constant_dynamic-update-slice_fusion.5
  498.9 0.8 constant_dynamic-update-slice_fusion.5
  503.0 0.8 constant_dynamic-update-slice_fusion.5
  507.1 0.8 constant_dynamic-update-slice_fusion.5
  511.2 0.8 constant_dynamic-update-slice_fusion.5
  515.3 0.8 constant_dynamic-update-slice_fusion.5
  519.4 0.8 constant_dynamic-update-slice_fusion.5
  523.5 0.8 constant_dynamic-update-slice_fusion.5
  527.6 0.8 constant_dynamic-update-slice_fusion.5
  531.7 0.8 constant_dynamic-update-slice_fusion.5
  535.8 0.8 constant_dynamic-update-slice_fusion.5
  539.9 0.8 constant_dynamic-update-slice_fusion.5
  542.4 267.9 %while.73 = (s32[]{:T(128)}, f32[2,64,64]{2,0,1:T(2,128)S(1)}, f32[2,64,64]{0,2,1:T(8,128)S(1)}, s32[]{:T(128)}, s32[2]{0:T(128)S(1)}, /*index=5*/s32[1]{0:T(128)}, s32[3]{0:T(128)S(1)}, s32[]{:T(128)}, s32[]{:T(128)}) while((s32[]{:T(128)}, f32[2,64,64]{2,0,1:T(2,128)S(1)}, f32[2,64,64]{0,2,1:T(8,128)S(1)}, s32[]{:T(128)}, ...), condition=%wide.region_14.15_spmd.clone, body=%wide.region_11.14_spmd.clone.sunk | while | flops 197400 | bytes 75255 | solution.py:40
  545.8 0.8 fusion.169
  811.8 267.9 %while.74 = (s32[]{:T(128)}, f32[2,64,64]{2,0,1:T(2,128)S(1)}, f32[2,64,64]{0,2,1:T(8,128)S(1)}, s32[]{:T(128)}, s32[2]{0:T(128)S(1)}, /*index=5*/s32[1]{0:T(128)}, s32[3]{0:T(128)S(1)}, s32[]{:T(128)}, s32[]{:T(128)}) while((s32[]{:T(128)}, f32[2,64,64]{2,0,1:T(2,128)S(1)}, f32[2,64,64]{0,2,1:T(8,128)S(1)}, s32[]{:T(128)}, ...), condition=%wide.region_18.19_spmd.clone, body=%wide.region_15.0_spmd.clone.sunk | while | flops 197400 | bytes 75255 | solution.py:40
  1082.3 0.8 reshape.449
  (2710 shorter events, 766.4 us)
Async XLA Ops:
  1.7 8.3 collective-permute-start
  7.7 6.6 collective-permute-start.1
  15.7 4.4 collective-permute-start.2
  17.0 4.0 collective-permute-start.3
  20.1 61.2 %copy-start = (s32[2]{0:T(128)S(1)}, s32[2]{0:T(128)}, u32[]{:S(2)}) copy-start(s32[2]{0:T(128)} %constant.357.clone.2) | copy-start | bytes 28
  20.1 61.2 %copy-start.1 = (s32[3]{0:T(128)S(1)}, s32[3]{0:T(128)}, u32[]{:S(2)}) copy-start(s32[3]{0:T(128)} %constant.358.clone.2) | copy-start | bytes 40
  81.2 328.1 %copy-start.2 = (s32[2]{0:T(128)S(1)}, s32[2]{0:T(128)}, u32[]{:S(2)}) copy-start(s32[2]{0:T(128)} %constant.365.clone.2) | copy-start | bytes 28
  81.2 328.1 %copy-start.3 = (s32[3]{0:T(128)S(1)}, s32[3]{0:T(128)}, u32[]{:S(2)}) copy-start(s32[3]{0:T(128)} %constant.366.clone.2) | copy-start | bytes 40
where the time goes:
time: 1090 us; the launch traced here: 1080 us
  other arithmetic  404 us (37%)
  local copies, waits for them, and re-layouts  308 us (28%)
  loops' own time  154 us (14%)
  blocking collectives  116 us (11%)
  matrix products  84 us (8%)
    while x448, local copies, waits for them, and re-layouts, row_step(): column = lax.dynamic_slice_in_dim(matrix, row, 1, 1)[:, 0]  286 us
    scatter x224, other arithmetic, row_step(): lax.dynamic_update_slice_in_dim(inverse, inverse_row[None], row, 0)  170 us
    another operation x224, other arithmetic  163 us
    another operation x4, loops' own time, cholesky_pair(): lax.fori_loop(0, order, row_step, (jnp.zeros_like(matrix), jnp.zeros_like...  154 us
    psum x1, blocking collectives, per_device(): sum_uu, sum_ua = lax.psum((local_uu, local_ua), ('lon', 'lat'))  58.7 us
    psum x1, blocking collectives, per_device(): sum_rr = lax.psum(local_rr, ('lon', 'lat'))  57.6 us
    dot_general x224, matrix products, row_step(): partial_row = jnp.dot(inverse, column, precision=FULL_PRECISION)  43.8 us
    dot_general x224, matrix products, row_step(): jnp.dot(partial_row, inverse, precision=FULL_PRECISION)  35.1 us
  transfers between devices with their start and end apart: 4, of which 2 were waited for; matrix products, arithmetic and copies ran while one was open for 0% of the time, Pallas kernels for 0%

commit v1 on v0

--- a/solution.py
+++ b/solution.py
@@ -104,7 +104,11 @@
     low_inverse, projected, lifted = jax.vmap(project_one)(sum_uu / cell_count, sum_ua / cell_count)
     residual = residual_rows(fields, basis_rows, lifted)
     local_rr = jnp.einsum("fsc,ftc->fst", residual, residual, precision=FULL_PRECISION)
-    sum_rr = lax.psum(local_rr, ("lon", "lat"))
+
+    def wires_plan(slab_in, axis_id):
+        return jnp.sum(jax.lax.all_gather(slab_in, axis_id), axis=0)
+
+    sum_rr = wires_plan(local_rr, ("lon", "lat"))
     factor_up, up_inverse = jax.vmap(upper_pair)(sum_rr / cell_count)
     mix_old, mix_new, new_values = jax.vmap(rotate_one)(
         low_inverse, projected, factor_up, up_inverse, old_values

time: 1090 us -> 1050 us (0.963)
  blocking collectives: 116 us -> 77.4 us
    psum x1 -> x0, blocking collectives: 57.6 us -> none  [per_device(): sum_rr = lax.psum(local_rr, ('lon', 'lat'))]
    all_gather x0 -> x1, blocking collectives: none -> 18.7 us  [wires_plan(): return jnp.sum(jax.lax.all_gather(slab_in, axis_id), axis=0)]
where the time goes in v1:
time: 1050 us; the launch traced here: 1040 us
  other arithmetic  404 us (38%)
  local copies, waits for them, and re-layouts  308 us (29%)
  loops' own time  154 us (15%)
  matrix products  84 us (8%)
  blocking collectives  77.4 us (7%)
    while x448, local copies, waits for them, and re-layouts, row_step(): column = lax.dynamic_slice_in_dim(matrix, row, 1, 1)[:, 0]  286 us
    scatter x224, other arithmetic, row_step(): lax.dynamic_update_slice_in_dim(inverse, inverse_row[None], row, 0)  170 us
    another operation x224, other arithmetic  163 us
    another operation x4, loops' own time, cholesky_pair(): lax.fori_loop(0, order, row_step, (jnp.zeros_like(matrix), jnp.zeros_like...  154 us
    psum x1, blocking collectives, per_device(): sum_uu, sum_ua = lax.psum((local_uu, local_ua), ('lon', 'lat'))  58.7 us
    dot_general x224, matrix products, row_step(): partial_row = jnp.dot(inverse, column, precision=FULL_PRECISION)  43.8 us
    dot_general x224, matrix products, row_step(): jnp.dot(partial_row, inverse, precision=FULL_PRECISION)  35.1 us
    reduce_sum x224, other arithmetic, row_step(): pivot = jnp.sqrt(diag_entry - jnp.sum(partial_row * partial_row))  30 us
  transfers between devices with their start and end apart: 4, of which 2 were waited for; matrix products, arithmetic and copies ran while one was open for 0% of the time, Pallas kernels for 0%

profile of v1, /device:TPU:0, one launch (start us, length us, event | category | flops | bytes accessed | tf_op | source)
XLA Modules:
  0.0 1044.2 jit_solution(2059523237273608825)
XLA Ops:
  0.6 1.0 fusion.76
  1.7 6.0 collective-permute-start
  7.7 1.1 reshape.448
  10.0 4.3 collective-permute-done.1
  14.3 1.2 fusion.47
  15.7 1.3 collective-permute-start.2
  17.0 3.0 collective-permute-start.3
  20.1 0.9 collective-permute-done.3
  21.7 58.7 %all-reduce.1 = (f32[2,64,64]{2,1,0:T(8,128)S(1)}, f32[2,64,32]{1,2,0:T(8,128)S(1)}) all-reduce(f32[2,64,64]{2,1,0:T(8,128)S(1)} %fusion.78, f32[2,64,32]{1,2,0:T(8,128)S(1)} %convolution_bitcast_fusion), channel_id=1, replica_groups=mesh['level'=2,'lon'=8,'lat'=2] {'lon','lat'}, use_global_device_ids=true, to_apply=%region_0.0 | all-reduce | flops 12288 | bytes 98304 | tf_op jit(solution)/shard_map/psum | solution.py:103
  81.2 268.9 %while.71 = (s32[]{:T(128)}, f32[2,64,64]{2,0,1:T(2,128)S(1)}, f32[2,64,64]{0,2,1:T(8,128)S(1)}, s32[]{:T(128)}, s32[2]{0:T(128)S(1)}, /*index=5*/s32[1]{0:T(128)}, s32[3]{0:T(128)S(1)}, s32[]{:T(128)}, s32[]{:T(128)}) while((s32[]{:T(128)}, f32[2,64,64]{2,0,1:T(2,128)S(1)}, f32[2,64,64]{0,2,1:T(8,128)S(1)}, s32[]{:T(128)}, ...), condition=%wide.region_4.5_spmd.clone, body=%wide.region_1.4_spmd.clone.sunk | while | flops 197400 | bytes 75255 | solution.py:40
  351.3 18.7 %all-gather = f32[32,32,32]{2,1,0:T(8,128)S(1)} all-gather(f32[2,32,32]{2,1,0:T(8,128)S(1)} %fusion.80), channel_id=2, replica_groups=mesh['level'=2,'lon'=8,'lat'=2] {'lon','lat'}, dimensions={0}, use_global_device_ids=true | all-gather | bytes 139264 | tf_op jit(solution)/shard_map/all_gather | solution.py:109
  370.4 131.4 %while.72 = (s32[]{:T(128)}, f32[2,32,32]{2,0,1:T(2,128)S(1)}, f32[2,32,32]{2,0,1:T(2,128)S(1)}, f32[2,32,32]{0,2,1:T(8,128)S(1)}, s32[]{:T(128)}, /*index=5*/s3...) while((s32[]{:T(128)}, f32[2,32,32]{2,0,1:T(2,128)S(1)}, ...), condition=%wide.region_10.11_spmd.clone, body=%wide.region_7.10_spmd.clone.sunk | while | flops 49752 | bytes 26751 | solution.py:40
  373.7 0.8 constant_dynamic-update-slice_fusion.5
  377.8 0.8 constant_dynamic-update-slice_fusion.5
  382.0 0.8 constant_dynamic-update-slice_fusion.5
  386.1 0.8 constant_dynamic-update-slice_fusion.5
  390.2 0.8 constant_dynamic-update-slice_fusion.5
  394.3 0.8 constant_dynamic-update-slice_fusion.5
  398.4 0.8 constant_dynamic-update-slice_fusion.5
  402.5 0.8 constant_dynamic-update-slice_fusion.5
  406.6 0.8 constant_dynamic-update-slice_fusion.5
  410.7 0.8 constant_dynamic-update-slice_fusion.5
  414.8 0.8 constant_dynamic-update-slice_fusion.5
  418.9 0.8 constant_dynamic-update-slice_fusion.5
  423.0 0.8 constant_dynamic-update-slice_fusion.5
  427.1 0.8 constant_dynamic-update-slice_fusion.5
  431.2 0.8 constant_dynamic-update-slice_fusion.5
  435.3 0.8 constant_dynamic-update-slice_fusion.5
  439.4 0.8 constant_dynamic-update-slice_fusion.5
  443.6 0.8 constant_dynamic-update-slice_fusion.5
  447.7 0.8 constant_dynamic-update-slice_fusion.5
  451.8 0.8 constant_dynamic-update-slice_fusion.5
  455.9 0.8 constant_dynamic-update-slice_fusion.5
  460.0 0.8 constant_dynamic-update-slice_fusion.5
  464.1 0.8 constant_dynamic-update-slice_fusion.5
  468.2 0.8 constant_dynamic-update-slice_fusion.5
  472.3 0.8 constant_dynamic-update-slice_fusion.5
  476.4 0.8 constant_dynamic-update-slice_fusion.5
  480.5 0.8 constant_dynamic-update-slice_fusion.5
  484.6 0.8 constant_dynamic-update-slice_fusion.5
  488.7 0.8 constant_dynamic-update-slice_fusion.5
  492.8 0.8 constant_dynamic-update-slice_fusion.5
  496.9 0.8 constant_dynamic-update-slice_fusion.5
  501.1 0.8 constant_dynamic-update-slice_fusion.5
  503.5 267.9 %while.73 = (s32[]{:T(128)}, f32[2,64,64]{2,0,1:T(2,128)S(1)}, f32[2,64,64]{0,2,1:T(8,128)S(1)}, s32[]{:T(128)}, s32[2]{0:T(128)S(1)}, /*index=5*/s32[1]{0:T(128)}, s32[3]{0:T(128)S(1)}, s32[]{:T(128)}, s32[]{:T(128)}) while((s32[]{:T(128)}, f32[2,64,64]{2,0,1:T(2,128)S(1)}, f32[2,64,64]{0,2,1:T(8,128)S(1)}, s32[]{:T(128)}, ...), condition=%wide.region_14.15_spmd.clone, body=%wide.region_11.14_spmd.clone.sunk | while | flops 197400 | bytes 75255 | solution.py:40
  507.0 0.8 fusion.169
  772.9 267.9 %while.74 = (s32[]{:T(128)}, f32[2,64,64]{2,0,1:T(2,128)S(1)}, f32[2,64,64]{0,2,1:T(8,128)S(1)}, s32[]{:T(128)}, s32[2]{0:T(128)S(1)}, /*index=5*/s32[1]{0:T(128)}, s32[3]{0:T(128)S(1)}, s32[]{:T(128)}, s32[]{:T(128)}) while((s32[]{:T(128)}, f32[2,64,64]{2,0,1:T(2,128)S(1)}, f32[2,64,64]{0,2,1:T(8,128)S(1)}, s32[]{:T(128)}, ...), condition=%wide.region_18.19_spmd.clone, body=%wide.region_15.0_spmd.clone.sunk | while | flops 197400 | bytes 75255 | solution.py:40
  1043.4 0.8 reshape.449
  (2711 shorter events, 766.5 us)
Async XLA Ops:
  1.7 8.3 collective-permute-start
  7.7 6.6 collective-permute-start.1
  15.7 4.4 collective-permute-start.2
  17.0 4.0 collective-permute-start.3
  20.1 61.1 %copy-start = (s32[2]{0:T(128)S(1)}, s32[2]{0:T(128)}, u32[]{:S(2)}) copy-start(s32[2]{0:T(128)} %constant.357.clone.2) | copy-start | bytes 28
  20.1 61.1 %copy-start.1 = (s32[3]{0:T(128)S(1)}, s32[3]{0:T(128)}, u32[]{:S(2)}) copy-start(s32[3]{0:T(128)} %constant.358.clone.2) | copy-start | bytes 40
  81.2 289.2 %copy-start.2 = (s32[2]{0:T(128)S(1)}, s32[2]{0:T(128)}, u32[]{:S(2)}) copy-start(s32[2]{0:T(128)} %constant.365.clone.2) | copy-start | bytes 28
  81.2 289.2 %copy-start.3 = (s32[3]{0:T(128)S(1)}, s32[3]{0:T(128)}, u32[]{:S(2)}) copy-start(s32[3]{0:T(128)} %constant.366.clone.2) | copy-start | bytes 40
